TPU v7x, 256 devices: a whole 4x4x8 slice. The times are simulated.
256 devices in a mesh: ri: 8 (over y, core), mu: 4 (over x), nu: 8 (over z).
Axes of the slice: x: 4, y: 4, z: 8, core: 2. Of those that a mesh axis runs over, the one named last changes fastest.
Arguments:
- three_center: bfloat16 [32, 2304, 128, 128], P('ri', ('mu', 'nu')), may hold values from -0.15625 to 0.15625
- block_pairs: int32 [2304, 2], P(('mu', 'nu')), may hold values from -1 to 95, as said below
- occ_factor: bfloat16 [12288, 128], P(('mu', 'nu')), may hold values from -6 to 6
- virt_density: bfloat16 [12288, 12288], P(('mu', 'nu'), 'ri'), may hold values from -0.0546875 to 0.0546875
- block_sizes: int32 [96], replicated, may hold values from 96 to 128
- occ_mask: int32 [96], replicated, may hold values 0 or 1
- virt_mask: int32 [96, 96], replicated, may hold values 0 or 1
Outputs:
- transformed: bfloat16 [32, 12288, 128], P('ri', ('mu', 'nu'))
Inputs may be any that keep to these rules, and one draw needn't show every extreme that they name: `block_pairs`: slots k in [d * 72, (d + 1) * 72) belong to device d of mu+nu; a live slot holds a mu block of that device's mu range (the range of 24 blocks of its mu index) and any nu block; empty slots hold -1 in both columns, and the live slots of a device come first. Every mu block appears in exactly 12 live slots, with distinct nu blocks. A device holds at most 72 live slots, and in every mu range some device holds exactly 72.
All inputs are finite; a program needn't handle non-finite values.
Results may differ from a plain program's by a relative error of at most 0.015.
Values may be sent and summed in bfloat16 or wider, within the bound.
A program may use at most 128 MiB of HBM per device.

v0:
```python
import jax
import jax.numpy as jnp
from jax import lax
from jax.sharding import PartitionSpec as P

BS = 128
NB = 96


def body(three_center, block_pairs, occ_factor, virt_density, block_sizes, occ_mask, virt_mask):
    rows_dev = virt_density.shape[0]
    occ_cols = occ_factor.shape[1]
    ri_rows = three_center.shape[0]
    blocks_mu = NB // lax.axis_size("mu")
    total_rows = NB * BS
    inside = jnp.arange(BS, dtype=jnp.int32)[None, :] < block_sizes[:, None]
    keep_occ = (inside & (occ_mask[:, None] > 0)).reshape(total_rows)
    gathered_occ = lax.all_gather(occ_factor, ("mu", "nu"), axis=0, tiled=True)
    occ_kept = jnp.where(keep_occ[:, None], gathered_occ, jnp.zeros((), jnp.bfloat16))
    mu_block = block_pairs[:, 0]
    nu_block = jnp.clip(block_pairs[:, 1], 0, NB - 1)
    slot_live = mu_block >= 0
    occ_blocks = occ_kept.reshape(NB, BS, occ_cols)[nu_block]
    products = jnp.einsum(
        "pkab,kbo->pkao", three_center, occ_blocks, preferred_element_type=jnp.float32
    )
    local_block = mu_block - lax.axis_index("mu") * blocks_mu
    segment_ids = jnp.where(slot_live, local_block, blocks_mu)

    def slot_sum(slab_products):
        return jax.ops.segment_sum(slab_products, segment_ids, num_segments=blocks_mu + 1)[
            :blocks_mu
        ]

    partial_value = jax.vmap(slot_sum)(products)
    partial_value = partial_value.reshape(ri_rows, blocks_mu * BS, occ_cols)
    virt_all = lax.all_gather(virt_density, "ri", axis=1, tiled=True)
    row_start = (lax.axis_index("mu") * lax.axis_size("nu") + lax.axis_index("nu")) * rows_dev
    row_ids = row_start + jnp.arange(rows_dev, dtype=jnp.int32)
    block_pick = (row_ids[:, None] // BS == jnp.arange(NB, dtype=jnp.int32)[None, :]).astype(
        jnp.float32
    )
    mask_rows = jnp.dot(block_pick, virt_mask.astype(jnp.float32)) > 0.5
    row_inside = lax.dynamic_slice_in_dim(inside.reshape(total_rows), row_start, rows_dev)
    keep_virt = (mask_rows[:, :, None] & inside[None, :, :] & row_inside[:, None, None]).reshape(
        rows_dev, total_rows
    )
    virt_kept = jnp.where(keep_virt, virt_all, jnp.zeros((), jnp.bfloat16))
    summed = lax.psum_scatter(
        partial_value.astype(jnp.bfloat16), "nu", scatter_dimension=1, tiled=True
    )
    result = jnp.einsum(
        "sm,pmo->pso",
        virt_kept,
        lax.all_gather(summed, ("mu", "nu"), axis=1, tiled=True),
        preferred_element_type=jnp.float32,
    )
    return result.astype(jnp.bfloat16)


def solution(mesh):
    in_specs = (
        P("ri", ("mu", "nu"), None, None),
        P(("mu", "nu"), None),
        P(("mu", "nu"), None),
        P(("mu", "nu"), "ri"),
        P(),
        P(),
        P(),
    )
    out_specs = P("ri", ("mu", "nu"), None)
    return jax.shard_map(body, mesh=mesh, in_specs=in_specs, out_specs=out_specs, check_vma=False)
```

profile of v0, /device:TPU:24, one launch (start us, length us, event | category | flops | bytes accessed | tf_op | source)
XLA Modules:
  0.0 418.5 jit_solution(11618415687132992076)
XLA Ops:
  7.4 0.7 all-gather.4.cloned.1.call-update
  8.1 0.8 fusion.26
  8.9 0.7 broadcast_compare_fusion
  9.6 0.7 bitcast_compare_fusion
  10.3 83.0 %all-gather.4.cloned.1.call-done = bf16[12288,128]{1,0:T(8,128)(2,1)} async-done(((bf16[384,128]{1,0:T(8,128)(2,1)}), bf16[12288,128]{1,0:T(8,128)(2,1)}) %all-gather.4.cloned.1.call-update) | async-done | bytes 3145744 | tf_op jit(solution)/shard_map/all_gather | solution.py:18
  93.3 8.4 %broadcast_select_fusion = bf16[12288,128]{1,0:T(8,128)(2,1)S(1)} fusion(bf16[12288,128]{1,0:T(8,128)(2,1)} %all-gather.4.cloned.1.call-done, pred[12288]{0:T(1024)(128)(4,1)S(1)} %get-tuple-element.8), kind=kLoop, calls=%fused_computation.15 | loop fusion | flops 1572864 | bytes 6303744 | tf_op jit(solution)/shard_map/jit(_where)/select_n | solution.py:19
  101.8 2.4 gather_fusion
  104.2 13.5 %fusion.9 = f32[72,4,128,128]{2,3,1,0:T(8,128)} fusion(bf16[4,72,128,128]{3,2,1,0:T(8,128)(2,1)} %param.7, bf16[72,128,128]{2,1,0:T(8,128)(2,1)} %gather_fusion), kind=kOutput, calls=%fused_computation.11 | convolution fusion | flops 1207959552 | bytes 30670848 | tf_op jit(solution)/shard_map/pkab,kbo->pkao/dot_general | solution.py:24
  117.7 18.6 %copy.19 = f32[72,4,128,128]{3,2,1,0:T(8,128)} copy(f32[72,4,128,128]{2,3,1,0:T(8,128)} %fusion.9) | data formatting | bytes 37748736 | tf_op jit(solution)/shard_map/pkab,kbo->pkao/transpose | solution.py:24
  136.4 3.5 broadcast_in_dim.21
  139.9 41.7 %scatter_fusion = f32[4,25,128,128]{3,2,1,0:T(8,128)} fusion(f32[4,25,128,128]{3,2,1,0:T(8,128)} %broadcast_in_dim.21, s32[72]{0:T(128)S(1)} %get-tuple-element.6, f32[72,4,128,128]{3,2,1,0:T(8,128)} %copy.19), kind=kCustom, calls=%fused_computation.1 | custom fusion | flops 4718592 | bytes 56623392 | tf_op jit(solution)/shard_map/vmap()/scatter-add | solution.py:31
  181.6 3.5 slice.19
  185.1 15.0 %copy.26 = bf16[4,3072,128]{2,0,1:T(4,128)(2,1)S(1)} copy(bf16[4,3072,128]{2,1,0:T(8,128)(2,1)S(1)} %bitcast.57) | data formatting | bytes 6291456
  200.2 2.2 copy.44
  202.4 0.5 all-gather.8.cloned.1.call-update
  203.2 42.8 %reduce-scatter.4.cloned.1.call-done = bf16[384,512]{1,0:T(8,128)(2,1)} async-done(((bf16[3072,512]{1,0:T(8,128)(2,1)}), bf16[384,512]{1,0:T(8,128)(2,1)}) %reduce-scatter.4.cloned.1.call-update) | async-done | bytes 393232
  246.0 1.1 reshape.109
  247.1 1.0 copy.27
  248.1 0.3 convolution_compare_fusion
  248.9 7.1 %all-gather.8.cloned.1.call-done = bf16[384,12288]{1,0:T(8,128)(2,1)} async-done(((bf16[384,1536]{1,0:T(8,128)(2,1)}), bf16[384,12288]{1,0:T(8,128)(2,1)}) %all-gather.8.cloned.1.call-update) | async-done | bytes 9437200 | tf_op jit(solution)/shard_map/all_gather | solution.py:37
  255.9 130.8 %all-gather.6.cloned.1.call-done = bf16[4,12288,128]{1,2,0:T(8,128)(2,1)} async-done(((bf16[4,384,128]{1,2,0:T(8,128)(2,1)}), bf16[4,12288,128]{1,2,0:T(8,128)(2,1)}) %all-gather.6.cloned.1.call-update) | async-done | bytes 12582928 | tf_op jit(solution)/shard_map/all_gather | solution.py:55
  386.8 6.7 %and.60 = pred[384,96,128]{2,1,0:T(32,128)(4,1)S(1)} broadcast(pred[384,96]{1,0:T(8,128)(4,1)S(1)} %copy.21), dimensions={0,1} | broadcast | bytes 4755456 | tf_op jit(solution)/shard_map/and | solution.py:45
  393.4 16.7 %fusion.17 = bf16[4,384,128]{1,2,0:T(8,128)(2,1)S(1)} fusion(bf16[4,12288,128]{1,2,0:T(8,128)(2,1)} %all-gather.6.cloned.1.call-done, bf16[384,12288]{1,0:T(8,128)(2,1)} %all-gather.8.cloned.1.call-done, pred[48,8,96,128]{3,2,1,0:T(32,128)(4,1)S(1)} %bitcast.60, pred[384]{0:T(512)(128)(4,1)S(1)} %dynamic_slice.3, pred[12288]{0:T(1024)(128)(4,1)S(1)} %bitcast_compare_fusion.1), kind=kOutput, calls=%fused_computation.18 | convolution fusion | flops 4846190592 | bytes 27144576 | tf_op jit(solution)/shard_map/sm,pmo->pso/dot_general | solution.py:52
  410.1 0.9 copy.22
  (16 shorter events, 0.8 us)
Async XLA Ops:
  7.4 86.0 %all-gather.4.cloned.1.call-start = ((), (), s32[]{:S(2)}) async-start(), calls=%async_computation.1 | async-start | bytes 3244032 | tf_op jit(solution)/shard_map/all_gather | solution.py:18
  8.1 237.9 %reduce-scatter.4.cloned.1.call-start = ((), (), s32[]{:S(2)}) async-start(), calls=%async_computation.4 | async-start | bytes 3538944
  202.3 45.8 %copy-start.1 = (s32[96,96]{1,0:T(8,128)S(1)}, s32[96,96]{1,0:T(8,128)}, u32[]{:S(2)}) copy-start(s32[96,96]{1,0:T(8,128)} %param.13) | copy-start | bytes 110596
  202.3 46.3 %copy-start = (s32[96]{0:T(128)S(1)}, s32[96]{0:T(128)}, u32[]{:S(2)}) copy-start(s32[96]{0:T(128)} %param.11) | copy-start | bytes 1156
  202.4 53.6 %all-gather.8.cloned.1.call-start = ((), (), s32[]{:S(2)}) async-start(), calls=%async_computation.3 | async-start | bytes 10616832 | tf_op jit(solution)/shard_map/all_gather | solution.py:37
  202.9 183.8 %all-gather.6.cloned.1.call-start = ((), (), s32[]{:S(2)}) async-start(), calls=%async_computation.2 | async-start | bytes 12976128 | tf_op jit(solution)/shard_map/all_gather | solution.py:55
Sparse Core Ops, SparseCore 0:
  10.8 82.5 all-gather.3
  202.5 43.4 reduce-scatter.3
Sparse Core Ops, SparseCore 1:
  204.7 51.2 all-gather.7
  258.3 128.4 all-gather.5
where the time goes:
time: 419 us
  waiting for transfers between devices  265 us (63%)
  local copies, waits for them, and re-layouts  55.4 us (13%)
  other arithmetic  52.4 us (13%)
  matrix products  30.5 us (7%)
  between operations  15 us (4%)
    all_gather x1, waiting for transfers between devices, body(): lax.all_gather(summed, ('mu', 'nu'), axis=1, tiled=True)  131 us
    all_gather x1, waiting for transfers between devices, body(): gathered_occ = lax.all_gather(occ_factor, ('mu', 'nu'), axis=0, tiled=True)  83 us
    unnamed x5, waiting for transfers between devices  44.1 us
    scatter-add x1, other arithmetic, slot_sum(): jax.ops.segment_sum(slab_products, segment_ids, num_segments=blocks_mu + 1)  41.7 us
    unnamed x8, local copies, waits for them, and re-layouts  19.3 us
    transpose x1, local copies, waits for them, and re-layouts, body(): jnp.einsum('pkab,kbo->pkao', three_center, occ_blocks, preferred_element_...  18.6 us
    dot_general x1, matrix products, body(): jnp.einsum('sm,pmo->pso', virt_kept, lax.all_gather(summed, ('mu', 'nu'),...  16.7 us
    dot_general x1, matrix products, body(): jnp.einsum('pkab,kbo->pkao', three_center, occ_blocks, preferred_element_...  13.5 us
  transfers between devices with their start and end apart: 4, of which 4 were waited for; matrix products, arithmetic and copies ran while one was open for 1% of the time, Pallas kernels for 0%

commit v1 on v0

v1 whole, which is shorter than its diff:
```python
import functools

import jax
import jax.numpy as jnp
from jax import lax
from jax.experimental import pallas as pl
from jax.experimental.pallas import tpu as pltpu
from jax.sharding import PartitionSpec as P

MESH = pl.DeviceIdType.MESH
BS = 128
STAGGER = 2
SLOTS_A_STEP = 8
MIB = 1 << 20


class Copies:
    def __init__(self, send, recv):
        self.send, self.recv, self.used = send, recv, 0
        self.started = []

    def make(self, src, dst, device):
        i = self.used
        self.used += 1
        return pltpu.make_async_remote_copy(
            src_ref=src,
            dst_ref=dst,
            send_sem=self.send.at[i],
            recv_sem=self.recv.at[i],
            device_id=device,
            device_id_type=MESH,
        )

    def go(self, src, dst, device):
        copy = self.make(src, dst, device)
        copy.start()
        self.started.append(copy)
        return copy

    def wait_sends(self):
        for copy in self.started:
            copy.wait_send()


def greet(devices):
    barrier = pltpu.get_barrier_semaphore()
    for device in devices:
        pl.semaphore_signal(barrier, inc=1, device_id=device, device_id_type=MESH)
    pl.semaphore_wait(barrier, len(devices))


def occ_copies(x_size, z_size):
    return 4 * (z_size // 2) // 2 + 4 * z_size + x_size


def gather_occ(cores, x_size, z_size, occ_ref, all_ref, send, recv):
    x, z, r = lax.axis_index("mu"), lax.axis_index("nu"), lax.axis_index("ri")
    c = lax.rem(r, cores)
    zp, zm = {"nu": lax.rem(z + 1, z_size)}, {"nu": lax.rem(z + z_size - 1, z_size)}
    x_up, x_down = lax.rem(x + 1, x_size), lax.rem(x + x_size - 1, x_size)
    x_far = lax.rem(x + 2, x_size)
    xp, xm = {"mu": x_up}, {"mu": x_down}
    sibling = {"ri": r + 1 - 2 * c}
    rows = occ_ref.shape[0] // cores
    mine = pl.ds(pl.multiple_of(c * rows, 16), rows)
    first = pl.ds(pl.multiple_of(c * rows, 16), rows // 2)
    second = pl.ds(pl.multiple_of(c * rows + rows // 2, 16), rows // 2)
    far = z_size // 2
    greet([zp, zm, xp, xm, sibling])
    copies = Copies(send, recv)

    def here(column, shard, part):
        return all_ref.at[column, shard, part]

    def along_x(shard):
        ref = here(x, shard, mine)
        return shard, copies.go(ref, ref, xp), copies.go(ref, ref, xm)

    def pass_on(sent):
        shard, up, down = sent
        up.wait_recv()
        ref = here(x_down, shard, first)
        one = copies.go(ref, ref, xp)
        down.wait_recv()
        ref = here(x_up, shard, second)
        return one, copies.go(ref, ref, xm)

    all_ref[x, z, mine, :] = occ_ref[mine, :]
    ups, downs, waiting, passed = [], [], [], []
    for t in range(far):
        behind, ahead = lax.rem(z + z_size - t, z_size), lax.rem(z + t, z_size)
        last = t == far - 1
        if t:
            ups[-1].wait_recv()
        ref = here(x, behind, first if last else mine)
        ups.append(copies.go(ref, ref, zp))
        if t:
            downs[-1].wait_recv()
        ref = here(x, ahead, second if last else mine)
        downs.append(copies.go(ref, ref, zm))
        new = [along_x(behind)]
        if t:
            new.append(along_x(ahead))
        for sent in waiting:
            passed.append(pass_on(sent))
        waiting = new
    ups[-1].wait_recv()
    downs[-1].wait_recv()
    waiting.append(along_x(lax.rem(z + far, z_size)))
    over = [copies.go(all_ref.at[x, :, mine], all_ref.at[x, :, mine], sibling)]
    for sent in waiting:
        passed.append(pass_on(sent))
    for column in (x_down, x_up):
        ref = all_ref.at[column, :, mine]
        over.append(copies.go(ref, ref, sibling))
    for one, two in passed:
        one.wait_recv()
        two.wait_recv()
    ref = all_ref.at[x_far, :, mine]
    over.append(copies.go(ref, ref, sibling))
    for copy in over:
        copy.wait_recv()
    copies.wait_sends()


def half_transform(
    pairs, sizes, occ_mask, virt_mask, three_ref, occ_ref, virt_ref, part_ref, kept_ref, total
):
    g = pl.program_id(0)
    p_rows, slots = three_ref.shape[0], three_ref.shape[1]
    blocks = total.shape[1]
    occ_cols = occ_ref.shape[-1]
    first_block = lax.axis_index("mu") * blocks
    row_blocks, col_blocks = virt_ref.shape[0] // BS, virt_ref.shape[1] // BS
    row_ids = lax.broadcasted_iota(jnp.int32, (BS, BS), 0)
    col_ids = lax.broadcasted_iota(jnp.int32, (BS, BS), 1)
    occ_rows = lax.broadcasted_iota(jnp.int32, (BS, occ_cols), 0)

    @pl.when(g == 0)
    def _():
        total[...] = jnp.zeros_like(total)

    for j in range(slots):
        k = g * slots + j
        mu, nu = pairs[k, 0], pairs[k, 1]

        @pl.when(mu >= 0)
        def _(j=j, mu=mu, nu=nu):
            kept_rows = jnp.where(occ_mask[nu] > 0, sizes[nu], 0)
            occ = jnp.where(occ_rows < kept_rows, occ_ref[nu].astype(jnp.float32), 0.0)
            product = jnp.dot(
                three_ref[:, j].reshape(p_rows * BS, BS),
                occ.astype(jnp.bfloat16),
                preferred_element_type=jnp.float32,
            )
            total[:, mu - first_block] += product.reshape(p_rows, BS, occ_cols)

    @pl.when(g < row_blocks)
    def _():
        s_block = (lax.axis_index("mu") * lax.axis_size("nu") + lax.axis_index("nu")) * row_blocks + g
        rows = pl.ds(pl.multiple_of(g * BS, BS), BS)
        for b in range(col_blocks):
            m_block = lax.axis_index("ri") * col_blocks + b
            cols = pl.ds(b * BS, BS)
            kept_rows = jnp.where(virt_mask[s_block, m_block] > 0, sizes[s_block], 0)
            keep = (row_ids < kept_rows) & (col_ids < sizes[m_block])
            kept = jnp.where(keep, virt_ref[rows, cols].astype(jnp.float32), 0.0)
            kept_ref[rows, cols] = kept.astype(jnp.bfloat16)

    @pl.when(g == pl.num_programs(0) - 1)
    def _():
        part_ref[...] = total[...].astype(jnp.bfloat16)


def exchange_copies(x_size, z_size):
    return x_size * (4 * (z_size // 2)) + x_size + 6 + x_size


def exchange(
    cores, x_size, z_size,
    part_ref, virt_ref, out_ref,
    tile, sums, reduced, half, partial, landed,
    send, recv, plane_send, plane_recv, out_send, out_recv, own_sem,
):
    x, z, r = lax.axis_index("mu"), lax.axis_index("nu"), lax.axis_index("ri")
    c, y = lax.rem(r, cores), r // cores
    y_size = x_size
    far = z_size // 2
    rows, occ_cols = part_ref.shape[2], part_ref.shape[3]
    zp, zm = {"nu": lax.rem(z + 1, z_size)}, {"nu": lax.rem(z + z_size - 1, z_size)}
    x_up, x_down = lax.rem(x + 1, x_size), lax.rem(x + x_size - 1, x_size)
    x_far = lax.rem(x + 2, x_size)
    xp, xm = {"mu": x_up}, {"mu": x_down}
    sibling = {"ri": r + 1 - 2 * c}
    first, second = pl.ds(0, rows // 2), pl.ds(rows // 2, rows // 2)
    sides = (first, second)
    plane = [
        {"ri": lax.rem(y + b, y_size) * cores + c, "mu": lax.rem(x + a, x_size)}
        for b in range(y_size)
        for a in range(x_size)
        if a or b
    ]
    greet([zp, zm, sibling] + plane)
    copies = Copies(send, recv)
    ahead = lambda t: lax.rem(z + t + z_size, z_size)
    towards = (zp, zm)
    chunks = range(x_size)
    which = [lax.rem(k - y + y_size, y_size) for k in chunks]
    itself = [(x == y) & (which[k] == x) for k in chunks]
    scattering = {}
    moving = {}
    gathering = {}
    leaving = []

    def scatter(t, k):
        for d in (0, 1):
            shard = ahead(far - t if d == 0 else t - far)
            if t == 0:
                src = part_ref.at[which[k], shard, sides[d]]
                dst = sums.at[d, k, 0, sides[d]]
            else:
                scattering[d, k, t - 1].wait_recv()
                src = sums.at[d, k, t - 1]
                dst = sums.at[d, k, t]
                if t == 1:
                    a, b = sides[d], sides[1 - d]
                    added = src[a, :].astype(jnp.float32) + part_ref[which[k], shard, a, :].astype(jnp.float32)
                    src[a, :] = added.astype(jnp.bfloat16)
                    src[b, :] = part_ref[which[k], shard, b, :]
                else:
                    added = src[...].astype(jnp.float32) + part_ref[which[k], shard].astype(jnp.float32)
                    src[...] = added.astype(jnp.bfloat16)
            scattering[d, k, t] = copies.go(src, dst, towards[d])

    def move(k):
        for d in (0, 1):
            scattering[d, k, far - 1].wait_recv()
        added = part_ref[which[k], z].astype(jnp.float32)
        added += sums[0, k, far - 1].astype(jnp.float32) + sums[1, k, far - 1].astype(jnp.float32)
        added = added.astype(jnp.bfloat16)
        copy = moving[k] = pltpu.make_async_remote_copy(
            src_ref=reduced.at[k],
            dst_ref=half.at[k, z],
            send_sem=plane_send.at[k],
            recv_sem=plane_recv.at[k],
            device_id={"ri": x * cores + c, "mu": which[k]},
            device_id_type=MESH,
        )

        @pl.when(itself[k])
        def _():
            half[k, z] = added

        @pl.when(jnp.logical_not(itself[k]))
        def _():
            reduced[k] = added
            copy.start()

    def gather(t, k):
        if t == 0:

            @pl.when(jnp.logical_not(itself[k]))
            def _():
                moving[k].wait_recv()

        for d in (0, 1):
            if t:
                gathering[d, k, t - 1].wait_recv()
            shard = ahead(-t if d == 0 else t)
            ref = half.at[k, shard, sides[d]] if t == far - 1 else half.at[k, shard]
            gathering[d, k, t] = copies.go(ref, ref, towards[d])

    def gathered(k):
        for d in (0, 1):
            gathering[d, k, far - 1].wait_recv()

    depth = z_size // cores
    width = depth * rows

    def product(k, turn):
        off = (2, 1, 3, 0)[turn]
        column = lax.rem(x + off, x_size)
        value = None
        for b in range(cores):
            shards = half[k, b * depth : (b + 1) * depth].reshape(width, occ_cols)
            term = jnp.dot(tile[column, b], shards, preferred_element_type=jnp.float32)
            value = term if value is None else value + term
        value = value.astype(jnp.bfloat16)
        to_y = lax.rem(k - x + y_size, y_size)
        copy = pltpu.make_async_remote_copy(
            src_ref=partial.at[k, off],
            dst_ref=landed.at[x, y],
            send_sem=out_send.at[k * x_size + off],
            recv_sem=out_recv.at[x * y_size + y],
            device_id={"ri": to_y * cores + c, "mu": column},
            device_id_type=MESH,
        )
        if off:
            partial[k, off] = value
            copy.start()
            leaving.append((None, copy))
            return
        remote = to_y != y

        @pl.when(remote)
        def _():
            partial[k, off] = value
            copy.start()

        @pl.when(jnp.logical_not(remote))
        def _():
            landed[x, y] = value

        leaving.append((remote, copy))

    def finish(k):
        i = which[k]
        for b in range(y_size):
            arrival = pltpu.make_async_remote_copy(
                src_ref=partial.at[k, 0],
                dst_ref=landed.at[i, b],
                send_sem=out_send.at[k * x_size],
                recv_sem=out_recv.at[i * y_size + b],
                device_id=zp,
                device_id_type=MESH,
            )

            @pl.when(jnp.logical_not((i == x) & (y == b)))
            def _(arrival=arrival):
                arrival.wait_recv()

        value = landed[i, 0].astype(jnp.float32)
        for b in range(1, y_size):
            value += landed[i, b].astype(jnp.float32)
        out_ref[i] = value.astype(jnp.bfloat16)

    virt = {}

    def virt_start():
        virt["own"] = pltpu.make_async_copy(virt_ref, tile.at[x, c], own_sem)
        virt["own"].start()
        for name, side, to in (("p0", 0, xp), ("m1", 1, xm), ("p1", 1, xp), ("m0", 0, xm)):
            virt[name] = copies.go(virt_ref.at[sides[side]], tile.at[x, c, sides[side]], to)

    def virt_pass():
        for name, side, of, to in (("p", 0, x_down, xp), ("m", 1, x_up, xm)):
            virt[f"{name}{side}"].wait_recv()
            ref = tile.at[of, c, sides[side]]
            virt[name] = copies.go(ref, ref, to)
        virt["own over"] = copies.go(virt_ref, tile.at[x, c], sibling)

    def virt_over():
        virt["p1"].wait_recv()
        virt["m0"].wait_recv()
        for of, name in ((x_down, "down over"), (x_up, "up over")):
            virt[name] = copies.go(tile.at[of, c], tile.at[of, c], sibling)

    def virt_far():
        virt["p"].wait_recv()
        virt["m"].wait_recv()
        virt["far over"] = copies.go(tile.at[x_far, c], tile.at[x_far, c], sibling)

    def virt_end():
        virt["own"].wait()
        for name in ("own over", "down over", "up over", "far over"):
            virt[name].wait_recv()

    ready = 2 * far + 1
    events = [(0.5, virt_start), (3.5, virt_pass), (6.5, virt_over), (ready - 0.5, virt_far), (ready + 0.15, virt_end)]
    for k in chunks:
        at = STAGGER * k + 0.01 * k
        for t in range(far):
            events.append((at + t, functools.partial(scatter, t, k)))
            events.append((at + far + 1 + t, functools.partial(gather, t, k)))
        events.append((at + far, functools.partial(move, k)))
        events.append((at + ready, functools.partial(gathered, k)))
        for turn in range(x_size):
            events.append((at + ready + 0.2 + 0.5 * turn, functools.partial(product, k, turn)))
        events.append((at + ready + 4, functools.partial(finish, k)))
    for _, event in sorted(events, key=lambda one: one[0]):
        event()
    copies.wait_sends()
    for k in chunks:

        @pl.when(jnp.logical_not(itself[k]))
        def _(k=k):
            moving[k].wait_send()

    for remote, copy in leaving:
        if remote is None:
            copy.wait_send()
        else:

            @pl.when(remote)
            def _(copy=copy):
                copy.wait_send()


def body(three_center, block_pairs, occ_factor, virt_density, block_sizes, occ_mask, virt_mask):
    x_size, z_size = lax.axis_size("mu"), lax.axis_size("nu")
    y_size = x_size
    cores = lax.axis_size("ri") // y_size
    far = z_size // 2
    rows, occ_cols = occ_factor.shape
    p_rows, slots = three_center.shape[:2]
    width = virt_density.shape[1]
    blocks = block_sizes.shape[0] // x_size
    vmem = pl.BlockSpec(memory_space=pltpu.VMEM)
    dma = pltpu.SemaphoreType.DMA

    count = occ_copies(x_size, z_size) + 2 * far
    occ_all = pl.pallas_call(
        functools.partial(gather_occ, cores, x_size, z_size),
        out_shape=jax.ShapeDtypeStruct((x_size, z_size, rows, occ_cols), jnp.bfloat16),
        in_specs=[vmem],
        out_specs=vmem,
        scratch_shapes=[dma((count,)), dma((count,))],
        compiler_params=pltpu.CompilerParams(
            collective_id=0, has_side_effects=True, vmem_limit_bytes=16 * MIB
        ),
        name="gather_occ",
    )(occ_factor)

    group = SLOTS_A_STEP
    part, kept = pl.pallas_call(
        half_transform,
        grid_spec=pltpu.PrefetchScalarGridSpec(
            num_scalar_prefetch=4,
            grid=(slots // group,),
            in_specs=[
                pl.BlockSpec((p_rows, group, BS, BS), lambda g, *_: (0, g, 0, 0)),
                vmem,
                vmem,
            ],
            out_specs=[vmem, vmem],
            scratch_shapes=[pltpu.VMEM((p_rows, blocks, BS, occ_cols), jnp.float32)],
        ),
        out_shape=[
            jax.ShapeDtypeStruct((p_rows, blocks, BS, occ_cols), jnp.bfloat16),
            jax.ShapeDtypeStruct(virt_density.shape, jnp.bfloat16),
        ],
        compiler_params=pltpu.CompilerParams(vmem_limit_bytes=40 * MIB),
        name="half_transform",
    )(
        block_pairs, block_sizes, occ_mask, virt_mask,
        three_center, occ_all.reshape(x_size * z_size * rows // BS, BS, occ_cols), virt_density,
    )

    count = 16 * x_size + 16
    part = part.reshape(p_rows, z_size, rows, occ_cols)
    return pl.pallas_call(
        functools.partial(exchange, cores, x_size, z_size),
        out_shape=jax.ShapeDtypeStruct((p_rows, rows, occ_cols), jnp.bfloat16),
        in_specs=[vmem, vmem],
        out_specs=vmem,
        scratch_shapes=[
            pltpu.VMEM((x_size, cores, rows, width), jnp.bfloat16),
            pltpu.VMEM((2, x_size, far, rows, occ_cols), jnp.bfloat16),
            pltpu.VMEM((x_size, rows, occ_cols), jnp.bfloat16),
            pltpu.VMEM((x_size, z_size, rows, occ_cols), jnp.bfloat16),
            pltpu.VMEM((x_size, x_size, rows, occ_cols), jnp.bfloat16),
            pltpu.VMEM((p_rows, y_size, rows, occ_cols), jnp.bfloat16),
            dma((count,)),
            dma((count,)),
            dma((x_size,)),
            dma((x_size,)),
            dma((x_size * x_size,)),
            dma((p_rows * y_size,)),
            dma,
        ],
        compiler_params=pltpu.CompilerParams(
            collective_id=1, has_side_effects=True, vmem_limit_bytes=48 * MIB
        ),
        name="exchange",
    )(part, kept)


def solution(mesh):
    in_specs = (
        P("ri", ("mu", "nu"), None, None),
        P(("mu", "nu"), None),
        P(("mu", "nu"), None),
        P(("mu", "nu"), "ri"),
        P(),
        P(),
        P(),
    )
    out_specs = P("ri", ("mu", "nu"), None)
    return jax.shard_map(body, mesh=mesh, in_specs=in_specs, out_specs=out_specs, check_vma=False)
```

time: 419 us -> 168 us (0.40)
  waiting for transfers between devices: 265 us -> 0 us
  Pallas kernels: 0 us -> 165 us
  local copies, waits for them, and re-layouts: 55.4 us -> 2.52 us
  other arithmetic: 52.4 us -> 0 us
  matrix products: 30.5 us -> 0 us
  between operations: 15 us -> 0.06 us
    all_gather x3 -> x0, waiting for transfers between devices: 221 us -> none  [the longest x1 131 us: body(): lax.all_gather(summed, ('mu', 'nu'), axis=1, tiled=True)]
    pallas_call x0 -> x3, Pallas kernels: none -> 165 us  [the longest x1 124 us: body(): pl.pallas_call(functools.partial(exchange, cores, x_size, z_size), out_sh...]
    unnamed x5 -> x0, waiting for transfers between devices: 44.1 us -> none
    scatter-add x1 -> x0, other arithmetic: 41.7 us -> none  [slot_sum(): jax.ops.segment_sum(slab_products, segment_ids, num_segments=blocks_mu + 1)]
    dot_general x3 -> x0, matrix products: 30.5 us -> none  [the longest x1 16.7 us: body(): jnp.einsum('sm,pmo->pso', virt_kept, lax.all_gather(summed, ('mu', 'nu'),...]
    transpose x1 -> x0, local copies, waits for them, and re-layouts: 18.6 us -> none  [body(): jnp.einsum('pkab,kbo->pkao', three_center, occ_blocks, preferred_element_...]
    unnamed x8 -> x12, local copies, waits for them, and re-layouts: 19.3 us -> 2.52 us
    select_n x3 -> x0, other arithmetic: 9.22 us -> none  [the longest x1 8.45 us: body(): jnp.where(keep_occ[:, None], gathered_occ, jnp.zeros((), jnp.bfloat16))]
  transfers between devices with their start and end apart: 4 -> 0, of which waited for: 4 -> 0; matrix products, arithmetic and copies ran while one was open for 1% -> 0% of each run, Pallas kernels for 0% -> 0%
where the time goes in v1:
time: 168 us
  Pallas kernels  165 us (98%)
  local copies, waits for them, and re-layouts  2.52 us (2%)
    pallas_call x1, Pallas kernels, body(): pl.pallas_call(functools.partial(exchange, cores, x_size, z_size), out_sh...  124 us
    pallas_call x1, Pallas kernels, body(): pl.pallas_call(functools.partial(gather_occ, cores, x_size, z_size), out_...  28.1 us
    pallas_call x1, Pallas kernels, body(): pl.pallas_call(half_transform, grid_spec=pltpu.PrefetchScalarGridSpec(num...  13.8 us

profile of v1, /device:TPU:24, one launch (start us, length us, event | category | flops | bytes accessed | tf_op | source)
XLA Modules:
  0.0 168.1 jit_solution(17345386522317204836)
XLA Ops:
  0.0 0.0 copy-start
  0.0 0.9 copy.8.pairs
  0.9 0.0 copy-start.1
  0.9 0.9 copy-done.1
  1.8 0.0 copy-start.2
  1.8 0.0 copy-start.3
  1.8 0.0 copy-start.4
  1.8 28.1 %gather_occ.1 = bf16[4,8,384,128]{3,2,1,0:T(8,128)(2,1)S(1)} custom-call(bf16[384,128]{1,0:T(8,128)(2,1)S(1)} %copy-done.1), custom_call_target="tpu_custom_call" | custom-call | tf_op jit(solution)/shard_map/gather_occ/pallas_call | solution.py:412
  29.8 0.0 copy-done
  29.8 0.0 copy-done.2
  29.8 0.0 copy-done.3
  29.9 0.0 copy-done.4
  29.9 13.8 %half_transform.1 = (bf16[4,24,128,128]{3,2,1,0:T(8,128)(2,1)S(1)}, bf16[384,1536]{1,0:T(8,128)(2,1)S(1)}) custom-call(s32[72,2]{1,0:T(8,128)S(1)} %copy.8.pairs, s32[96]{0:T(128)S(1)} %copy-done.3, s32[96]{0:T(128)S(1)} %copy-done.4, s32[96,96]{1,0:T(8,128)S(1)} %copy-done.2, bf16[4,72,128,128]{3,2,1,0:T(8,128)(2,1)} %three_ref.1, ...), custom_call_target="tpu_custom_call" | custom-call | tf_op jit(solution)/shard_map/half_transform/pallas_call | solution.py:425
  43.6 123.7 %exchange.1 = bf16[4,384,128]{2,1,0:T(8,128)(2,1)S(1)} custom-call(bf16[4,8,384,128]{3,2,1,0:T(8,128)(2,1)S(1)} %bitcast.3, bf16[384,1536]{1,0:T(8,128)(2,1)S(1)} %get-tuple-element.8.virt_ref), custom_call_target="tpu_custom_call" | custom-call | tf_op jit(solution)/shard_map/exchange/pallas_call | solution.py:451
  167.3 0.7 copy.10
Async XLA Ops:
  0.0 29.8 %copy-start = (bf16[384,1536]{1,0:T(8,128)(2,1)S(1)}, bf16[384,1536]{1,0:T(8,128)(2,1)}, u32[]{:S(2)}) copy-start(bf16[384,1536]{1,0:T(8,128)(2,1)} %virt_ref.1) | copy-start | bytes 3538948
  0.9 0.9 copy-start.1
  1.8 28.1 %copy-start.2 = (s32[96,96]{1,0:T(8,128)S(1)}, s32[96,96]{1,0:T(8,128)}, u32[]{:S(2)}) copy-start(s32[96,96]{1,0:T(8,128)} %virt_mask.1) | copy-start | bytes 110596
  1.8 28.1 %copy-start.3 = (s32[96]{0:T(128)S(1)}, s32[96]{0:T(128)}, u32[]{:S(2)}) copy-start(s32[96]{0:T(128)} %sizes.1) | copy-start | bytes 1156
  1.8 28.1 %copy-start.4 = (s32[96]{0:T(128)S(1)}, s32[96]{0:T(128)}, u32[]{:S(2)}) copy-start(s32[96]{0:T(128)} %occ_mask.1) | copy-start | bytes 1156

commit v2 on v0

v2 whole, which is shorter than its diff:
```python
import functools

import jax
import jax.numpy as jnp
from jax import lax
from jax.experimental import pallas as pl
from jax.experimental.pallas import tpu as pltpu
from jax.sharding import PartitionSpec as P

MESH = pl.DeviceIdType.MESH
BS = 128
STAGGER = 1
VIRT_TIMES = (0.3, 1.4, 5.4)
SLOTS_A_STEP = 8
MIB = 1 << 20


class Copies:
    def __init__(self, send, recv):
        self.send, self.recv, self.used = send, recv, 0
        self.started = []

    def make(self, src, dst, device):
        i = self.used
        self.used += 1
        return pltpu.make_async_remote_copy(
            src_ref=src,
            dst_ref=dst,
            send_sem=self.send.at[i],
            recv_sem=self.recv.at[i],
            device_id=device,
            device_id_type=MESH,
        )

    def go(self, src, dst, device):
        copy = self.make(src, dst, device)
        copy.start()
        self.started.append(copy)
        return copy

    def wait_sends(self):
        for copy in self.started:
            copy.wait_send()


def greet(devices):
    barrier = pltpu.get_barrier_semaphore()
    for device in devices:
        pl.semaphore_signal(barrier, inc=1, device_id=device, device_id_type=MESH)
    pl.semaphore_wait(barrier, len(devices))


def chain_slots(x_size, subs, pairs, prev, last, nu_of):
    slots, blocks = pairs.shape[0], last.shape[0] - 1
    first_block = lax.axis_index("mu") * blocks

    def clear(b, _):
        last[b] = slots
        return 0

    def link(k, _):
        mu = pairs[k, 0]
        block = jnp.where(mu >= 0, mu - first_block, blocks)
        prev[k] = last[block]
        last[block] = k
        nu = jnp.maximum(pairs[k, 1], 0)
        inner = lax.rem(nu, blocks)
        nu_of[k] = (lax.div(inner, subs) * x_size + lax.div(nu, blocks)) * subs + lax.rem(inner, subs)
        return 0

    lax.fori_loop(0, blocks + 1, clear, 0)
    lax.fori_loop(0, slots, link, 0)


def transform(
    cores, x_size, z_size,
    prev, last, nu_of, sizes, occ_mask, virt_mask,
    three_hbm, occ_ref, virt_ref, out_ref,
    occ_all, three, chain, part, kept, tile, sums, reduced, half, partial, landed,
    send, recv, plane_send, plane_recv, out_send, out_recv, own_sem, three_sem,
):
    x, z, r = lax.axis_index("mu"), lax.axis_index("nu"), lax.axis_index("ri")
    c, y = lax.rem(r, cores), r // cores
    y_size = x_size
    far = z_size // 2
    slots, occ_cols = prev.shape[0], occ_ref.shape[-1]
    subs = occ_ref.shape[0]
    rows = subs * BS
    zp, zm = {"nu": lax.rem(z + 1, z_size)}, {"nu": lax.rem(z + z_size - 1, z_size)}
    x_up, x_down = lax.rem(x + 1, x_size), lax.rem(x + x_size - 1, x_size)
    x_far = lax.rem(x + 2, x_size)
    xp, xm = {"mu": x_up}, {"mu": x_down}
    sibling = {"ri": r + 1 - 2 * c}
    ahead = lambda t: lax.rem(z + t + z_size, z_size)
    towards = (zp, zm)
    chunks = range(x_size)
    which = [lax.rem(k - y + y_size, y_size) for k in chunks]
    loads = [pltpu.make_async_copy(three_hbm.at[which[k]], three.at[k], three_sem.at[k]) for k in chunks]
    for load in loads:
        load.start()
    plane = [
        {"ri": lax.rem(y + b, y_size) * cores + c, "mu": lax.rem(x + a, x_size)}
        for b in range(y_size)
        for a in range(x_size)
        if a or b
    ]
    greet([zp, zm, sibling] + plane)
    copies = Copies(send, recv)
    bf16, f32 = jnp.bfloat16, jnp.float32

    span = BS // cores
    mine = pl.ds(pl.multiple_of(c * span, 16), span)
    lower = pl.ds(pl.multiple_of(c * span, 16), span // 2)
    upper = pl.ds(pl.multiple_of(c * span + span // 2, 16), span // 2)

    def here(column, shard, some):
        return occ_all.at[pl.ds((shard * x_size + column) * subs, subs), some]

    def across(shard):
        ref = occ_all.at[pl.ds(shard * x_size * subs, x_size * subs), mine]
        over.append(copies.go(ref, ref, sibling))

    over = []
    rising, falling = {}, {}

    def along_z(column, t):
        final = t == far - 1
        if t:
            rising[t - 1, column].wait_recv()
        ref = here(columns[column], ahead(-t), lower if final else mine)
        rising[t, column] = copies.go(ref, ref, zp)
        if t:
            falling[t - 1, column].wait_recv()
        ref = here(columns[column], ahead(t), upper if final else mine)
        falling[t, column] = copies.go(ref, ref, zm)

    columns = (x, x_down, x_up, x_far)
    own_block = (x * z_size + z) * subs
    occ_rows = lax.broadcasted_iota(jnp.int32, (span, occ_cols), 0) + c * span
    for b in range(subs):
        kept_rows = jnp.where(occ_mask[own_block + b] > 0, sizes[own_block + b], 0)
        occ_kept = jnp.where(occ_rows < kept_rows, occ_ref[b, mine, :].astype(f32), 0.0)
        occ_all[(z * x_size + x) * subs + b, mine, :] = occ_kept.astype(bf16)

    def mask_virt():
        row_ids = lax.broadcasted_iota(jnp.int32, (BS, BS), 0)
        col_ids = lax.broadcasted_iota(jnp.int32, (BS, BS), 1)
        col_blocks = virt_ref.shape[1] // BS
        for a in range(subs):
            for b in range(col_blocks):
                m_block = r * col_blocks + b
                kept_rows = jnp.where(virt_mask[own_block + a, m_block] > 0, sizes[own_block + a], 0)
                keep = (row_ids < kept_rows) & (col_ids < sizes[m_block])
                at = pl.ds(a * BS, BS), pl.ds(b * BS, BS)
                kept[at] = jnp.where(keep, virt_ref[at].astype(f32), 0.0).astype(bf16)

    virt = {}
    first, second = pl.ds(0, rows // 2), pl.ds(rows // 2, rows // 2)
    sides = (first, second)

    def virt_start():
        virt["own"] = pltpu.make_async_copy(kept, tile.at[x, c], own_sem)
        virt["own"].start()
        for name, side, to in (("p0", 0, xp), ("m1", 1, xm), ("p1", 1, xp), ("m0", 0, xm)):
            virt[name] = copies.go(kept.at[sides[side]], tile.at[x, c, sides[side]], to)

    def virt_pass():
        for name, side, of, to in (("p", 0, x_down, xp), ("m", 1, x_up, xm)):
            virt[f"{name}{side}"].wait_recv()
            ref = tile.at[of, c, sides[side]]
            virt[name] = copies.go(ref, ref, to)
        virt["own over"] = copies.go(kept, tile.at[x, c], sibling)

    def virt_over():
        virt["p1"].wait_recv()
        virt["m0"].wait_recv()
        for of, name in ((x_down, "down over"), (x_up, "up over")):
            virt[name] = copies.go(tile.at[of, c], tile.at[of, c], sibling)

    def virt_far():
        virt["p"].wait_recv()
        virt["m"].wait_recv()
        virt["far over"] = copies.go(tile.at[x_far, c], tile.at[x_far, c], sibling)

    def virt_end():
        virt["own"].wait()
        for name in ("own over", "down over", "up over", "far over"):
            virt[name].wait_recv()

    ref = here(x, z, mine)
    from_down, from_up = copies.go(ref, ref, xp), copies.go(ref, ref, xm)
    along_z(0, 0)
    mask_virt()
    chain[slots] = jnp.zeros(chain.shape[1:], f32)
    from_down.wait_recv()
    ref = here(x_down, z, lower)
    far_lower = copies.go(ref, ref, xp)
    from_up.wait_recv()
    ref = here(x_up, z, upper)
    far_upper = copies.go(ref, ref, xm)
    virt_start()
    along_z(1, 0)
    along_z(2, 0)
    far_lower.wait_recv()
    far_upper.wait_recv()
    along_z(3, 0)
    across(z)
    for t in range(1, far):
        for column in range(x_size):
            along_z(column, t)
        across(ahead(-t))
        across(ahead(t))
    for column in range(x_size):
        rising[far - 1, column].wait_recv()
        falling[far - 1, column].wait_recv()
    across(ahead(far))
    for copy in over:
        copy.wait_recv()

    itself = [(x == y) & (which[k] == x) for k in chunks]
    halves = (pl.ds(0, BS // 2), pl.ds(BS // 2, BS // 2))
    scattering, moving, gathering, leaving = {}, {}, {}, []

    def slot_sums(k):
        loads[k].wait()

        def some_slots(g, _):
            for j in range(SLOTS_A_STEP):
                slot = g * SLOTS_A_STEP + j
                product = jnp.dot(three[k, slot], occ_all[nu_of[slot]], preferred_element_type=f32)
                chain[slot] = product + chain[prev[slot]]
            return 0

        def one_shard(shard, _):
            for b in range(subs):
                part[k, shard, b] = chain[last[shard * subs + b]].astype(bf16)
            return 0

        lax.fori_loop(0, slots // SLOTS_A_STEP, some_slots, 0)
        lax.fori_loop(0, z_size, one_shard, 0)

    def scatter(t, k):
        for d in (0, 1):
            shard = ahead(far - t if d == 0 else t - far)
            a, b = halves[d], halves[1 - d]
            if t == 0:
                src = part.at[k, shard, :, a]
                dst = sums.at[d, k, 0, :, a]
            else:
                scattering[d, k, t - 1].wait_recv()
                src = sums.at[d, k, t - 1]
                dst = sums.at[d, k, t]
                if t == 1:
                    added = src[:, a, :].astype(f32) + part[k, shard, :, a, :].astype(f32)
                    src[:, a, :] = added.astype(bf16)
                    src[:, b, :] = part[k, shard, :, b, :]
                else:
                    added = src[...].astype(f32) + part[k, shard].astype(f32)
                    src[...] = added.astype(bf16)
            scattering[d, k, t] = copies.go(src, dst, towards[d])

    def move(k):
        for d in (0, 1):
            scattering[d, k, far - 1].wait_recv()
        added = part[k, z].astype(f32)
        added += sums[0, k, far - 1].astype(f32) + sums[1, k, far - 1].astype(f32)
        added = added.astype(bf16)
        copy = moving[k] = pltpu.make_async_remote_copy(
            src_ref=reduced.at[k],
            dst_ref=half.at[k, z],
            send_sem=plane_send.at[k],
            recv_sem=plane_recv.at[k],
            device_id={"ri": x * cores + c, "mu": which[k]},
            device_id_type=MESH,
        )

        @pl.when(itself[k])
        def _():
            half[k, z] = added

        @pl.when(jnp.logical_not(itself[k]))
        def _():
            reduced[k] = added
            copy.start()

    def gather(t, k):
        if t == 0:

            @pl.when(jnp.logical_not(itself[k]))
            def _():
                moving[k].wait_recv()

        for d in (0, 1):
            if t:
                gathering[d, k, t - 1].wait_recv()
            shard = ahead(-t if d == 0 else t)
            ref = half.at[k, shard, :, halves[d]] if t == far - 1 else half.at[k, shard]
            gathering[d, k, t] = copies.go(ref, ref, towards[d])

    def gathered(k):
        for d in (0, 1):
            gathering[d, k, far - 1].wait_recv()

    depth = z_size // cores

    def product(k, turn):
        off = (2, 1, 3, 0)[turn]
        column = lax.rem(x + off, x_size)
        value = None
        for b in range(cores):
            shards = half[k, b * depth : (b + 1) * depth].reshape(depth * rows, occ_cols)
            term = jnp.dot(tile[column, b], shards, preferred_element_type=f32)
            value = term if value is None else value + term
        value = value.astype(bf16)
        to_y = lax.rem(k - x + y_size, y_size)
        copy = pltpu.make_async_remote_copy(
            src_ref=partial.at[k, off],
            dst_ref=landed.at[x, y],
            send_sem=out_send.at[k * x_size + off],
            recv_sem=out_recv.at[x * y_size + y],
            device_id={"ri": to_y * cores + c, "mu": column},
            device_id_type=MESH,
        )
        if off:
            partial[k, off] = value
            copy.start()
            leaving.append((None, copy))
            return
        remote = to_y != y

        @pl.when(remote)
        def _():
            partial[k, off] = value
            copy.start()

        @pl.when(jnp.logical_not(remote))
        def _():
            landed[x, y] = value

        leaving.append((remote, copy))

    def finish(k):
        i = which[k]
        for b in range(y_size):
            arrival = pltpu.make_async_remote_copy(
                src_ref=partial.at[k, 0],
                dst_ref=landed.at[i, b],
                send_sem=out_send.at[k * x_size],
                recv_sem=out_recv.at[i * y_size + b],
                device_id=zp,
                device_id_type=MESH,
            )

            @pl.when(jnp.logical_not((i == x) & (y == b)))
            def _(arrival=arrival):
                arrival.wait_recv()

        value = landed[i, 0].astype(f32)
        for b in range(1, y_size):
            value += landed[i, b].astype(f32)
        out_ref[i] = value.astype(bf16)

    ready = 2 * far + 1
    events = [
        (VIRT_TIMES[0], virt_pass), (VIRT_TIMES[1], virt_over), (VIRT_TIMES[2], virt_far), (ready + 0.15, virt_end)
    ]
    for k in chunks:
        at = STAGGER * k + 0.01 * k
        events.append((at - 0.5, functools.partial(slot_sums, k)))
        for t in range(far):
            events.append((at + t, functools.partial(scatter, t, k)))
            events.append((at + far + 1 + t, functools.partial(gather, t, k)))
        events.append((at + far, functools.partial(move, k)))
        events.append((at + ready, functools.partial(gathered, k)))
        for turn in range(x_size):
            events.append((at + ready + 0.2 + 0.3 * turn, functools.partial(product, k, turn)))
        events.append((at + ready + 4, functools.partial(finish, k)))
    for _, event in sorted(events, key=lambda one: one[0]):
        event()
    copies.wait_sends()
    for k in chunks:

        @pl.when(jnp.logical_not(itself[k]))
        def _(k=k):
            moving[k].wait_send()

    for remote, copy in leaving:
        if remote is None:
            copy.wait_send()
        else:

            @pl.when(remote)
            def _(copy=copy):
                copy.wait_send()


def body(three_center, block_pairs, occ_factor, virt_density, block_sizes, occ_mask, virt_mask):
    x_size, z_size = lax.axis_size("mu"), lax.axis_size("nu")
    y_size = x_size
    cores = lax.axis_size("ri") // y_size
    far = z_size // 2
    rows, occ_cols = occ_factor.shape
    subs = rows // BS
    p_rows, slots = three_center.shape[:2]
    width = virt_density.shape[1]
    blocks = block_sizes.shape[0] // x_size
    vmem = pl.BlockSpec(memory_space=pltpu.VMEM)
    smem = pl.BlockSpec(memory_space=pltpu.SMEM)
    dma = pltpu.SemaphoreType.DMA
    bf16 = jnp.bfloat16

    prev, last, nu_of = pl.pallas_call(
        functools.partial(chain_slots, x_size, subs),
        out_shape=[jax.ShapeDtypeStruct((n,), jnp.int32) for n in (slots, blocks + 1, slots)],
        in_specs=[smem],
        out_specs=[smem] * 3,
        name="chain_slots",
    )(block_pairs)

    shard = (subs, BS, occ_cols)
    count = 6 * far * x_size + z_size + 14
    out = pl.pallas_call(
        functools.partial(transform, cores, x_size, z_size),
        out_shape=jax.ShapeDtypeStruct((p_rows, rows, occ_cols), bf16),
        in_specs=[smem] * 6 + [pl.BlockSpec(memory_space=pl.ANY), vmem, vmem],
        out_specs=vmem,
        scratch_shapes=[
            pltpu.VMEM((x_size * blocks, BS, occ_cols), bf16),
            pltpu.VMEM((p_rows, slots, BS, BS), bf16),
            pltpu.VMEM((slots + 1, BS, occ_cols), jnp.float32),
            pltpu.VMEM((p_rows, z_size) + shard, bf16),
            pltpu.VMEM((rows, width), bf16),
            pltpu.VMEM((x_size, cores, rows, width), bf16),
            pltpu.VMEM((2, x_size, far) + shard, bf16),
            pltpu.VMEM((x_size,) + shard, bf16),
            pltpu.VMEM((x_size, z_size) + shard, bf16),
            pltpu.VMEM((x_size, x_size, rows, occ_cols), bf16),
            pltpu.VMEM((p_rows, y_size, rows, occ_cols), bf16),
            dma((count,)),
            dma((count,)),
            dma((x_size,)),
            dma((x_size,)),
            dma((x_size * x_size,)),
            dma((p_rows * y_size,)),
            dma,
            dma((p_rows,)),
        ],
        compiler_params=pltpu.CompilerParams(
            collective_id=0, has_side_effects=True, vmem_limit_bytes=56 * MIB
        ),
        name="transform",
    )(
        prev, last, nu_of, block_sizes, occ_mask, virt_mask,
        three_center, occ_factor.reshape(shard), virt_density,
    )
    return out


def solution(mesh):
    in_specs = (
        P("ri", ("mu", "nu"), None, None),
        P(("mu", "nu"), None),
        P(("mu", "nu"), None),
        P(("mu", "nu"), "ri"),
        P(),
        P(),
        P(),
    )
    out_specs = P("ri", ("mu", "nu"), None)
    return jax.shard_map(body, mesh=mesh, in_specs=in_specs, out_specs=out_specs, check_vma=False)
```

time: 419 us -> 131 us (0.31)
  waiting for transfers between devices: 265 us -> 0 us
  Pallas kernels: 0 us -> 128 us
  other arithmetic: 52.4 us -> 0 us
  local copies, waits for them, and re-layouts: 55.4 us -> 3.15 us
  matrix products: 30.5 us -> 0 us
  between operations: 15 us -> 0.02 us
    all_gather x3 -> x0, waiting for transfers between devices: 221 us -> none  [the longest x1 131 us: body(): lax.all_gather(summed, ('mu', 'nu'), axis=1, tiled=True)]
    pallas_call x0 -> x2, Pallas kernels: none -> 128 us  [the longest x1 124 us: body(): pl.pallas_call(functools.partial(transform, cores, x_size, z_size), out_s...]
    unnamed x5 -> x0, waiting for transfers between devices: 44.1 us -> none
    scatter-add x1 -> x0, other arithmetic: 41.7 us -> none  [slot_sum(): jax.ops.segment_sum(slab_products, segment_ids, num_segments=blocks_mu + 1)]
    dot_general x3 -> x0, matrix products: 30.5 us -> none  [the longest x1 16.7 us: body(): jnp.einsum('sm,pmo->pso', virt_kept, lax.all_gather(summed, ('mu', 'nu'),...]
    transpose x1 -> x0, local copies, waits for them, and re-layouts: 18.6 us -> none  [body(): jnp.einsum('pkab,kbo->pkao', three_center, occ_blocks, preferred_element_...]
    unnamed x8 -> x2, local copies, waits for them, and re-layouts: 19.3 us -> 3.15 us
    select_n x3 -> x0, other arithmetic: 9.22 us -> none  [the longest x1 8.45 us: body(): jnp.where(keep_occ[:, None], gathered_occ, jnp.zeros((), jnp.bfloat16))]
  transfers between devices with their start and end apart: 4 -> 0, of which waited for: 4 -> 0; matrix products, arithmetic and copies ran while one was open for 1% -> 0% of each run, Pallas kernels for 0% -> 0%
where the time goes in v2:
time: 131 us
  Pallas kernels  128 us (98%)
  local copies, waits for them, and re-layouts  3.15 us (2%)
    pallas_call x1, Pallas kernels, body(): pl.pallas_call(functools.partial(transform, cores, x_size, z_size), out_s...  124 us
    pallas_call x1, Pallas kernels, body(): pl.pallas_call(functools.partial(chain_slots, x_size, subs), out_shape=[j...  3.39 us
    unnamed x2, local copies, waits for them, and re-layouts  3.15 us

profile of v2, /device:TPU:24, one launch (start us, length us, event | category | flops | bytes accessed | tf_op | source)
XLA Modules:
  0.0 131.0 jit_solution(17276187825621361633)
XLA Ops:
  0.0 1.4 %copy.8.pairs = s32[72,2]{1,0:T(8,128)} copy(s32[72,2]{0,1:T(2,128)} %param.8) | data formatting | bytes 1152 | tf_op args[1]
  1.4 3.4 %chain_slots.1 = (s32[72]{0:T(128)}, s32[25]{0:T(128)}, s32[72]{0:T(128)}) custom-call(s32[72,2]{1,0:T(8,128)} %copy.8.pairs), custom_call_target="tpu_custom_call" | custom-call | tf_op jit(solution)/shard_map/chain_slots/pallas_call | solution.py:412
  4.8 124.4 %transform.1 = bf16[4,384,128]{2,1,0:T(8,128)(2,1)} custom-call(s32[72]{0:T(128)} %get-tuple-element.8.prev, s32[25]{0:T(128)} %get-tuple-element.9.last, s32[72]{0:T(128)} %get-tuple-element.10.nu_of, s32[96]{0:T(128)} %sizes.1, s32[96]{0:T(128)} %occ_mask.1, s32[96,96]{1,0:T(8,128)} %virt_mask.1, bf16[4,72,128,128]{3,2,1,0:T(8,128)(2,1)} %three_hbm.1, ...), custom_call_target="tpu_custom_call" | custom-call | tf_op jit(solution)/shard_map/transform/pallas_call | solution.py:422
  129.2 1.8 %copy.10 = bf16[4,384,128]{2,1,0:T(8,128)(2,1)} copy(bf16[4,384,128]{2,1,0:T(8,128)(2,1)} %transform.1) | data formatting | bytes 786432

commit v3 on v2

--- a/solution.py
+++ b/solution.py
@@ -9,8 +9,8 @@
 
 MESH = pl.DeviceIdType.MESH
 BS = 128
-STAGGER = 1
-VIRT_TIMES = (0.3, 1.4, 5.4)
+STARTS = (0, 0.5, 1.5, 2.5)
+VIRT_TIMES = (2.4, 2.6, 6.4, 8.4)
 SLOTS_A_STEP = 8
 MIB = 1 << 20
 
@@ -50,40 +50,45 @@
     pl.semaphore_wait(barrier, len(devices))
 
 
-def chain_slots(x_size, subs, pairs, prev, last, nu_of):
-    slots, blocks = pairs.shape[0], last.shape[0] - 1
+def chain_slots(blocks, x_size, subs, slots, pairs_ref, padded, rows_ref):
+    lanes = padded.shape[1]
+    padded[...] = jnp.full(padded.shape, -1, jnp.int32)
+    padded[:, : pairs_ref.shape[1]] = pairs_ref[...]
     first_block = lax.axis_index("mu") * blocks
-
-    def clear(b, _):
-        last[b] = slots
-        return 0
-
-    def link(k, _):
-        mu = pairs[k, 0]
-        block = jnp.where(mu >= 0, mu - first_block, blocks)
-        prev[k] = last[block]
-        last[block] = k
-        nu = jnp.maximum(pairs[k, 1], 0)
-        inner = lax.rem(nu, blocks)
-        nu_of[k] = (lax.div(inner, subs) * x_size + lax.div(nu, blocks)) * subs + lax.rem(inner, subs)
-        return 0
-
-    lax.fori_loop(0, blocks + 1, clear, 0)
-    lax.fori_loop(0, slots, link, 0)
+    mu = jnp.broadcast_to(padded[0:1, :] - first_block, (lanes, lanes))
+    mu_down = mu.astype(jnp.float32).T.astype(jnp.int32)
+    down = lax.broadcasted_iota(jnp.int32, (lanes, lanes), 0)
+    along = lax.broadcasted_iota(jnp.int32, (lanes, lanes), 1)
+    before = jnp.where((mu == mu_down) & (down < along), down, -1)
+    prev = jnp.max(before, axis=0, keepdims=True)
+    ends = jnp.max(jnp.where(mu_down == along, down, -1), axis=0, keepdims=True)
+    nu = jnp.maximum(padded[1:2, :], 0)
+    column, shard = jnp.zeros_like(nu), jnp.zeros_like(nu)
+    for i in range(1, x_size):
+        column += jnp.where(nu >= i * blocks, 1, 0)
+    inner = nu - column * blocks
+    for i in range(1, blocks // subs):
+        shard += jnp.where(inner >= i * subs, 1, 0)
+    sub = inner - shard * subs
+    rows_ref[0:1, :] = jnp.where(prev < 0, slots, prev)
+    rows_ref[1:2, :] = jnp.where(ends < 0, slots, ends)
+    rows_ref[3:8, :] = jnp.zeros((5, lanes), jnp.int32)
+    rows_ref[2:3, :] = (shard * x_size + column) * subs + sub
 
 
 def transform(
     cores, x_size, z_size,
-    prev, last, nu_of, sizes, occ_mask, virt_mask,
-    three_hbm, occ_ref, virt_ref, out_ref,
-    occ_all, three, chain, part, kept, tile, sums, reduced, half, partial, landed,
+    sizes, occ_mask, virt_mask,
+    pairs_ref, three_hbm, occ_ref, virt_ref, out_ref,
+    occ_all, three, chain, part, kept, tile, total, summed, sums, reduced, half, partial, landed,
     send, recv, plane_send, plane_recv, out_send, out_recv, own_sem, three_sem,
+    padded, plan_rows, plan, plan_sem,
 ):
     x, z, r = lax.axis_index("mu"), lax.axis_index("nu"), lax.axis_index("ri")
     c, y = lax.rem(r, cores), r // cores
     y_size = x_size
     far = z_size // 2
-    slots, occ_cols = prev.shape[0], occ_ref.shape[-1]
+    slots, occ_cols = three_hbm.shape[1], occ_ref.shape[-1]
     subs = occ_ref.shape[0]
     rows = subs * BS
     zp, zm = {"nu": lax.rem(z + 1, z_size)}, {"nu": lax.rem(z + z_size - 1, z_size)}
@@ -94,7 +99,7 @@
     ahead = lambda t: lax.rem(z + t + z_size, z_size)
     towards = (zp, zm)
     chunks = range(x_size)
-    which = [lax.rem(k - y + y_size, y_size) for k in chunks]
+    which = [lax.rem(k - y - x + 2 * y_size, y_size) for k in chunks]
     loads = [pltpu.make_async_copy(three_hbm.at[which[k]], three.at[k], three_sem.at[k]) for k in chunks]
     for load in loads:
         load.start()
@@ -158,29 +163,36 @@
     first, second = pl.ds(0, rows // 2), pl.ds(rows // 2, rows // 2)
     sides = (first, second)
 
+    NEXT, FAR, BEFORE = 1, 2, 3
+
+    def strip(distance, side=None):
+        at, size = distance * rows, rows
+        if side is not None:
+            at, size = at + side * (rows // 2), rows // 2
+        return tile.at[c, pl.ds(at, size)]
+
     def virt_start():
-        virt["own"] = pltpu.make_async_copy(kept, tile.at[x, c], own_sem)
+        virt["own"] = pltpu.make_async_copy(kept, strip(0), own_sem)
         virt["own"].start()
-        for name, side, to in (("p0", 0, xp), ("m1", 1, xm), ("p1", 1, xp), ("m0", 0, xm)):
-            virt[name] = copies.go(kept.at[sides[side]], tile.at[x, c, sides[side]], to)
+        for name, side, lands, to in (("p0", 0, BEFORE, xp), ("m1", 1, NEXT, xm), ("p1", 1, BEFORE, xp), ("m0", 0, NEXT, xm)):
+            virt[name] = copies.go(kept.at[sides[side]], strip(lands, side), to)
 
     def virt_pass():
-        for name, side, of, to in (("p", 0, x_down, xp), ("m", 1, x_up, xm)):
+        for name, side, of, to in (("p", 0, BEFORE, xp), ("m", 1, NEXT, xm)):
             virt[f"{name}{side}"].wait_recv()
-            ref = tile.at[of, c, sides[side]]
-            virt[name] = copies.go(ref, ref, to)
-        virt["own over"] = copies.go(kept, tile.at[x, c], sibling)
+            virt[name] = copies.go(strip(of, side), strip(FAR, side), to)
+        virt["own over"] = copies.go(kept, strip(0), sibling)
 
     def virt_over():
         virt["p1"].wait_recv()
         virt["m0"].wait_recv()
-        for of, name in ((x_down, "down over"), (x_up, "up over")):
-            virt[name] = copies.go(tile.at[of, c], tile.at[of, c], sibling)
+        for of, name in ((BEFORE, "down over"), (NEXT, "up over")):
+            virt[name] = copies.go(strip(of), strip(of), sibling)
 
     def virt_far():
         virt["p"].wait_recv()
         virt["m"].wait_recv()
-        virt["far over"] = copies.go(tile.at[x_far, c], tile.at[x_far, c], sibling)
+        virt["far over"] = copies.go(strip(FAR), strip(FAR), sibling)
 
     def virt_end():
         virt["own"].wait()
@@ -188,22 +200,20 @@
             virt[name].wait_recv()
 
     ref = here(x, z, mine)
-    from_down, from_up = copies.go(ref, ref, xp), copies.go(ref, ref, xm)
+    from_down, from_up, from_far = [copies.go(ref, ref, to) for to in (xp, xm, {"mu": x_far})]
     along_z(0, 0)
     mask_virt()
     chain[slots] = jnp.zeros(chain.shape[1:], f32)
+    chain_slots(z_size * subs, x_size, subs, slots, pairs_ref, padded, plan_rows)
+    planning = pltpu.make_async_copy(plan_rows, plan, plan_sem)
+    planning.start()
     from_down.wait_recv()
-    ref = here(x_down, z, lower)
-    far_lower = copies.go(ref, ref, xp)
+    along_z(1, 0)
     from_up.wait_recv()
-    ref = here(x_up, z, upper)
-    far_upper = copies.go(ref, ref, xm)
+    along_z(2, 0)
+    from_far.wait_recv()
+    along_z(3, 0)
     virt_start()
-    along_z(1, 0)
-    along_z(2, 0)
-    far_lower.wait_recv()
-    far_upper.wait_recv()
-    along_z(3, 0)
     across(z)
     for t in range(1, far):
         for column in range(x_size):
@@ -216,6 +226,7 @@
     across(ahead(far))
     for copy in over:
         copy.wait_recv()
+    planning.wait()
 
     itself = [(x == y) & (which[k] == x) for k in chunks]
     halves = (pl.ds(0, BS // 2), pl.ds(BS // 2, BS // 2))
@@ -227,13 +238,13 @@
         def some_slots(g, _):
             for j in range(SLOTS_A_STEP):
                 slot = g * SLOTS_A_STEP + j
-                product = jnp.dot(three[k, slot], occ_all[nu_of[slot]], preferred_element_type=f32)
-                chain[slot] = product + chain[prev[slot]]
+                product = jnp.dot(three[k, slot], occ_all[plan[2, slot]], preferred_element_type=f32)
+                chain[slot] = product + chain[plan[0, slot]]
             return 0
 
         def one_shard(shard, _):
             for b in range(subs):
-                part[k, shard, b] = chain[last[shard * subs + b]].astype(bf16)
+                part[k, shard, b] = chain[plan[1, shard * subs + b]].astype(bf16)
             return 0
 
         lax.fori_loop(0, slots // SLOTS_A_STEP, some_slots, 0)
@@ -303,16 +314,36 @@
 
     depth = z_size // cores
 
-    def product(k, turn):
-        off = (2, 1, 3, 0)[turn]
-        column = lax.rem(x + off, x_size)
+    def shard_term(k, distance, at=0, size=x_size * rows):
+        shard = ahead(distance)
+        cols = pl.ds(pl.multiple_of(lax.rem(shard, depth) * rows, BS), rows)
+        return jnp.dot(
+            tile[shard // depth, at : at + size, cols],
+            half[k, shard].reshape(rows, occ_cols),
+            preferred_element_type=f32,
+        )
+
+    def grow(k, distances):
+        for distance in distances:
+            term = shard_term(k, distance)
+            total[...] = term if distance == 0 else total[...] + term
+
+    def whole(k):
         value = None
         for b in range(cores):
             shards = half[k, b * depth : (b + 1) * depth].reshape(depth * rows, occ_cols)
-            term = jnp.dot(tile[column, b], shards, preferred_element_type=f32)
+            term = jnp.dot(tile[b], shards, preferred_element_type=f32)
             value = term if value is None else value + term
+        total[...] = value
+
+    def product(k, turn):
+        off = (FAR, NEXT, BEFORE, 0)[turn]
+        column = lax.rem(x + off, x_size)
+        value = total[off * rows : (off + 1) * rows]
+        if k == x_size - 1:
+            value = value + shard_term(k, far, off * rows, rows)
         value = value.astype(bf16)
-        to_y = lax.rem(k - x + y_size, y_size)
+        to_y = which[k]
         copy = pltpu.make_async_remote_copy(
             src_ref=partial.at[k, off],
             dst_ref=landed.at[x, y],
@@ -340,8 +371,8 @@
         leaving.append((remote, copy))
 
     def finish(k):
-        i = which[k]
         for b in range(y_size):
+            i = lax.rem(k - y - b + 2 * y_size, y_size)
             arrival = pltpu.make_async_remote_copy(
                 src_ref=partial.at[k, 0],
                 dst_ref=landed.at[i, b],
@@ -355,26 +386,33 @@
             def _(arrival=arrival):
                 arrival.wait_recv()
 
-        value = landed[i, 0].astype(f32)
-        for b in range(1, y_size):
-            value += landed[i, b].astype(f32)
-        out_ref[i] = value.astype(bf16)
+            value = landed[i, b].astype(f32)
+            if k:
+                value = value + summed[i]
+            if k < x_size - 1:
+                summed[i] = value
+            else:
+                out_ref[i] = value.astype(bf16)
 
     ready = 2 * far + 1
     events = [
-        (VIRT_TIMES[0], virt_pass), (VIRT_TIMES[1], virt_over), (VIRT_TIMES[2], virt_far), (ready + 0.15, virt_end)
+        (VIRT_TIMES[0], virt_pass), (VIRT_TIMES[1], virt_over), (VIRT_TIMES[2], virt_far), (VIRT_TIMES[3], virt_end)
     ]
     for k in chunks:
-        at = STAGGER * k + 0.01 * k
+        at = STARTS[k] + 0.01 * k
         events.append((at - 0.5, functools.partial(slot_sums, k)))
         for t in range(far):
             events.append((at + t, functools.partial(scatter, t, k)))
             events.append((at + far + 1 + t, functools.partial(gather, t, k)))
+            if k == x_size - 1:
+                events.append((max(at + far + 1 + t, STARTS[k - 1] + ready + 0.3) + 0.05, functools.partial(grow, k, (-t, t) if t else (0,))))
         events.append((at + far, functools.partial(move, k)))
         events.append((at + ready, functools.partial(gathered, k)))
+        if k < x_size - 1:
+            events.append((at + ready + 0.1, functools.partial(whole, k)))
         for turn in range(x_size):
-            events.append((at + ready + 0.2 + 0.3 * turn, functools.partial(product, k, turn)))
-        events.append((at + ready + 4, functools.partial(finish, k)))
+            events.append((at + ready + 0.2 + 0.01 * turn, functools.partial(product, k, turn)))
+        events.append((at + ready + 3, functools.partial(finish, k)))
     for _, event in sorted(events, key=lambda one: one[0]):
         event()
     copies.wait_sends()
@@ -409,20 +447,12 @@
     dma = pltpu.SemaphoreType.DMA
     bf16 = jnp.bfloat16
 
-    prev, last, nu_of = pl.pallas_call(
-        functools.partial(chain_slots, x_size, subs),
-        out_shape=[jax.ShapeDtypeStruct((n,), jnp.int32) for n in (slots, blocks + 1, slots)],
-        in_specs=[smem],
-        out_specs=[smem] * 3,
-        name="chain_slots",
-    )(block_pairs)
-
     shard = (subs, BS, occ_cols)
     count = 6 * far * x_size + z_size + 14
     out = pl.pallas_call(
         functools.partial(transform, cores, x_size, z_size),
         out_shape=jax.ShapeDtypeStruct((p_rows, rows, occ_cols), bf16),
-        in_specs=[smem] * 6 + [pl.BlockSpec(memory_space=pl.ANY), vmem, vmem],
+        in_specs=[smem] * 3 + [vmem, pl.BlockSpec(memory_space=pl.ANY), vmem, vmem],
         out_specs=vmem,
         scratch_shapes=[
             pltpu.VMEM((x_size * blocks, BS, occ_cols), bf16),
@@ -430,7 +460,9 @@
             pltpu.VMEM((slots + 1, BS, occ_cols), jnp.float32),
             pltpu.VMEM((p_rows, z_size) + shard, bf16),
             pltpu.VMEM((rows, width), bf16),
-            pltpu.VMEM((x_size, cores, rows, width), bf16),
+            pltpu.VMEM((cores, x_size * rows, width), bf16),
+            pltpu.VMEM((x_size * rows, occ_cols), jnp.float32),
+            pltpu.VMEM((p_rows, rows, occ_cols), jnp.float32),
             pltpu.VMEM((2, x_size, far) + shard, bf16),
             pltpu.VMEM((x_size,) + shard, bf16),
             pltpu.VMEM((x_size, z_size) + shard, bf16),
@@ -444,14 +476,18 @@
             dma((p_rows * y_size,)),
             dma,
             dma((p_rows,)),
+            pltpu.VMEM((2, BS), jnp.int32),
+            pltpu.VMEM((8, BS), jnp.int32),
+            pltpu.SMEM((8, BS), jnp.int32),
+            dma,
         ],
         compiler_params=pltpu.CompilerParams(
             collective_id=0, has_side_effects=True, vmem_limit_bytes=56 * MIB
         ),
         name="transform",
     )(
-        prev, last, nu_of, block_sizes, occ_mask, virt_mask,
-        three_center, occ_factor.reshape(shard), virt_density,
+        block_sizes, occ_mask, virt_mask,
+        block_pairs.T, three_center, occ_factor.reshape(shard), virt_density,
     )
     return out
 

time: 131 us -> 122 us (0.931)
  Pallas kernels: 128 us -> 119 us
  local copies, waits for them, and re-layouts: 3.15 us -> 1.77 us
    pallas_call x1, Pallas kernels: 124 us -> 119 us  [body(): pl.pallas_call(functools.partial(transform, cores, x_size, z_size), out_s...]
    pallas_call x1 -> x0, Pallas kernels: 3.39 us -> none  [body(): pl.pallas_call(functools.partial(chain_slots, x_size, subs), out_shape=[j...]
    unnamed x2 -> x1, local copies, waits for them, and re-layouts: 3.15 us -> 1.77 us
where the time goes in v3:
time: 122 us; the launch traced here: 121 us
  Pallas kernels  119 us (98%)
  local copies, waits for them, and re-layouts  1.77 us (1%)
    pallas_call x1, Pallas kernels, body(): pl.pallas_call(functools.partial(transform, cores, x_size, z_size), out_s...  119 us

profile of v3, /device:TPU:24, one launch (start us, length us, event | category | flops | bytes accessed | tf_op | source)
XLA Modules:
  0.0 121.1 jit_solution(15132900087658188802)
XLA Ops:
  0.0 119.3 %transform.1 = bf16[4,384,128]{2,1,0:T(8,128)(2,1)} custom-call(s32[96]{0:T(128)} %sizes.1, s32[96]{0:T(128)} %occ_mask.1, s32[96,96]{1,0:T(8,128)} %virt_mask.1, s32[2,72]{1,0:T(2,128)} %bitcast.3, bf16[4,72,128,128]{3,2,1,0:T(8,128)(2,1)} %three_hbm.1, bf16[3,128,128]{2,1,0:T(8,128)(2,1)} %bitcast.2, bf16[384,1536]{1,0:T(8,128)(2,1)} %virt_ref.1), custom_call_target="tpu_custom_call" | custom-call | tf_op jit(solution)/shard_map/transform/pallas_call | solution.py:452
  119.3 1.8 %copy.9 = bf16[4,384,128]{2,1,0:T(8,128)(2,1)} copy(bf16[4,384,128]{2,1,0:T(8,128)(2,1)} %transform.1) | data formatting | bytes 786432

commit v4 on v3

--- a/solution.py
+++ b/solution.py
@@ -11,7 +11,7 @@
 BS = 128
 STARTS = (0, 0.5, 1.5, 2.5)
 VIRT_TIMES = (2.4, 2.6, 6.4, 8.4)
-SLOTS_A_STEP = 8
+SLOTS_A_STEP = 18
 MIB = 1 << 20
 
 
@@ -394,6 +394,23 @@
             else:
                 out_ref[i] = value.astype(bf16)
 
+    def sent():
+        copies.wait_sends()
+        for k in chunks:
+
+            @pl.when(jnp.logical_not(itself[k]))
+            def _(k=k):
+                moving[k].wait_send()
+
+        for remote, copy in leaving:
+            if remote is None:
+                copy.wait_send()
+            else:
+
+                @pl.when(remote)
+                def _(copy=copy):
+                    copy.wait_send()
+
     ready = 2 * far + 1
     events = [
         (VIRT_TIMES[0], virt_pass), (VIRT_TIMES[1], virt_over), (VIRT_TIMES[2], virt_far), (VIRT_TIMES[3], virt_end)
@@ -413,23 +430,9 @@
         for turn in range(x_size):
             events.append((at + ready + 0.2 + 0.01 * turn, functools.partial(product, k, turn)))
         events.append((at + ready + 3, functools.partial(finish, k)))
+    events.append((STARTS[-1] + ready + 2.9, sent))
     for _, event in sorted(events, key=lambda one: one[0]):
         event()
-    copies.wait_sends()
-    for k in chunks:
-
-        @pl.when(jnp.logical_not(itself[k]))
-        def _(k=k):
-            moving[k].wait_send()
-
-    for remote, copy in leaving:
-        if remote is None:
-            copy.wait_send()
-        else:
-
-            @pl.when(remote)
-            def _(copy=copy):
-                copy.wait_send()
 
 
 def body(three_center, block_pairs, occ_factor, virt_density, block_sizes, occ_mask, virt_mask):

time: 122 us -> 120 us (0.984)
    pallas_call x1, Pallas kernels: 119 us -> 118 us  [body(): pl.pallas_call(functools.partial(transform, cores, x_size, z_size), out_s...]
where the time goes in v4:
time: 120 us; the launch traced here: 119 us
  Pallas kernels  118 us (98%)
  local copies, waits for them, and re-layouts  1.77 us (1%)
    pallas_call x1, Pallas kernels, body(): pl.pallas_call(functools.partial(transform, cores, x_size, z_size), out_s...  118 us

profile of v4, /device:TPU:24, one launch (start us, length us, event | category | flops | bytes accessed | tf_op | source)
XLA Modules:
  0.0 119.4 jit_solution(15716649255007894090)
XLA Ops:
  0.0 117.6 %transform.1 = bf16[4,384,128]{2,1,0:T(8,128)(2,1)} custom-call(s32[96]{0:T(128)} %sizes.1, s32[96]{0:T(128)} %occ_mask.1, s32[96,96]{1,0:T(8,128)} %virt_mask.1, s32[2,72]{1,0:T(2,128)} %bitcast.3, bf16[4,72,128,128]{3,2,1,0:T(8,128)(2,1)} %three_hbm.1, bf16[3,128,128]{2,1,0:T(8,128)(2,1)} %bitcast.2, bf16[384,1536]{1,0:T(8,128)(2,1)} %virt_ref.1), custom_call_target="tpu_custom_call" | custom-call | tf_op jit(solution)/shard_map/transform/pallas_call | solution.py:455
  117.6 1.8 %copy.9 = bf16[4,384,128]{2,1,0:T(8,128)(2,1)} copy(bf16[4,384,128]{2,1,0:T(8,128)(2,1)} %transform.1) | data formatting | bytes 786432
